TPU v7x, 32 devices: a whole 2x2x4 slice. The times are simulated.
32 devices in a mesh: clip: 4 (over z), frame: 2 (over x), mp: 4 (over y, core).
Axes of the slice: x: 2, y: 2, z: 4, core: 2. Of those that a mesh axis runs over, the one named last changes fastest.
Arguments:
- query_spatial: bfloat16 [4, 2, 2, 40, 2560], P('clip', 'frame', None, None, 'mp'), may hold values from -24 to 24
- key_spatial: bfloat16 [4, 2, 2, 40, 2560], P('clip', 'frame', None, None, 'mp'), may hold values from -24 to 24
- value_spatial: bfloat16 [4, 2, 2, 40, 2560], P('clip', 'frame', None, None, 'mp'), may hold values from -10 to 10
- gains: float32 [3, 2560], P(None, 'mp'), may hold values from 0.5 to 2.5
- warp_lists: int32 [4, 2, 2], P('clip', 'frame'), may hold values from 0 to 1
- cotangent: bfloat16 [4, 2, 2, 40, 2560], P('clip', None, 'frame', None, 'mp'), may hold values from -3 to 3
Outputs:
- temporal_out: bfloat16 [4, 2, 2, 40, 2560], P('clip', None, 'frame', None, 'mp')
- grad_query: bfloat16 [4, 2, 2, 40, 2560], P('clip', 'frame', None, None, 'mp')
- grad_key: bfloat16 [4, 2, 2, 40, 2560], P('clip', 'frame', None, None, 'mp')
- grad_value: bfloat16 [4, 2, 2, 40, 2560], P('clip', 'frame', None, None, 'mp')
- grad_gains: float32 [3, 2560], P(None, 'mp')
All inputs are finite; a program needn't handle non-finite values.
Results may differ from a plain program's by a relative error of at most 0.035.
Values may be sent and summed in bfloat16 or wider, within the bound.
A program may use at most 128 MiB of HBM per device.

v0:
```python
import math

import jax
import jax.numpy as jnp
from jax import lax
from jax.sharding import PartitionSpec as P

HEADS = 20
HD = 128


epsilon = 1e-06


def attend_weights(queries, key_rows, visible):
    head_dim = queries.shape[-1]
    scores = jnp.einsum(
        "qhd,khd->hqk", queries, key_rows, preferred_element_type=jnp.float32
    ) / math.sqrt(head_dim)
    scores = jnp.where(visible[None], scores, -1e30)
    top = jnp.max(scores, axis=-1, keepdims=True)
    expon = jnp.exp(scores - top)
    return expon / jnp.sum(expon, axis=-1, keepdims=True)


def attend_forward(queries, key_rows, value_rows, visible):
    rounded = attend_weights(queries, key_rows, visible).astype(jnp.bfloat16)
    output = jnp.einsum("hqk,khd->qhd", rounded, value_rows, preferred_element_type=jnp.float32)
    return output.astype(jnp.bfloat16)


def attend_backward(queries, key_rows, value_rows, upstream, visible):
    head_dim = queries.shape[-1]
    weights = attend_weights(queries, key_rows, visible)
    rounded = weights.astype(jnp.bfloat16)
    grad_weights = jnp.einsum(
        "qhd,khd->hqk", upstream, value_rows, preferred_element_type=jnp.float32
    )
    inner = jnp.sum(weights * grad_weights, axis=-1, keepdims=True)
    grad_scores = (weights * (grad_weights - inner) / math.sqrt(head_dim)).astype(jnp.bfloat16)
    grad_queries = jnp.einsum(
        "hqk,khd->qhd", grad_scores, key_rows, preferred_element_type=jnp.float32
    )
    grad_keys = jnp.einsum("hqk,qhd->khd", grad_scores, queries, preferred_element_type=jnp.float32)
    grad_values = jnp.einsum("hqk,qhd->khd", rounded, upstream, preferred_element_type=jnp.float32)
    return (grad_queries, grad_keys, grad_values)


def scaled(array, gain):
    return (array.astype(jnp.float32) * gain).astype(jnp.bfloat16)


def body(query_spatial, key_spatial, value_spatial, gains, warp_lists, cotangent):
    tiles = query_spatial.shape[2]
    tile_tok = query_spatial.shape[3]
    local_width = query_spatial.shape[4]
    frames = cotangent.shape[1]
    heads_here = local_width // HD
    count = tiles * tile_tok
    frame_shape = (1, 1, tiles, tile_tok, local_width)
    tile_shape = (1, frames, 1, tile_tok, local_width)
    total_width = HEADS * HD
    gain_query = gains[0]
    gain_key = gains[1]
    gain_value = gains[2]

    def to_heads(array):
        return array.reshape(-1, heads_here, HD)

    all_visible = jnp.ones((count, count), bool)
    spatial = attend_forward(
        to_heads(query_spatial), to_heads(key_spatial), to_heads(value_spatial), all_visible
    )
    spatial_f = spatial.reshape(frame_shape).astype(jnp.float32)
    square_sum = lax.psum(jnp.sum(spatial_f * spatial_f, axis=-1, keepdims=True), "mp")
    inverse = lax.rsqrt(square_sum / total_width + epsilon)
    normed = (spatial_f * inverse).astype(jnp.bfloat16)
    warped = normed[:, :, warp_lists[0, 0]]
    tile_normed, tile_warped = (
        lax.all_to_all(normed, "frame", split_axis=2, concat_axis=1, tiled=True),
        lax.all_to_all(warped, "frame", split_axis=2, concat_axis=1, tiled=True),
    )
    tile_query = scaled(tile_normed, gain_query)
    tile_key = scaled(tile_warped, gain_key)
    tile_value = scaled(tile_warped, gain_value)
    frame_of = jnp.arange(frames * tile_tok) // tile_tok
    causal = frame_of[:, None] >= frame_of[None, :]
    temporal = attend_forward(
        to_heads(tile_query), to_heads(tile_key), to_heads(tile_value), causal
    )
    temporal_out = temporal.reshape(tile_shape)
    grad_tq, grad_tk, grad_tv = attend_backward(
        to_heads(tile_query), to_heads(tile_key), to_heads(tile_value), to_heads(cotangent), causal
    )
    grad_tq = grad_tq.reshape(tile_shape).astype(jnp.bfloat16)
    grad_tk = grad_tk.reshape(tile_shape).astype(jnp.bfloat16)
    grad_tv = grad_tv.reshape(tile_shape).astype(jnp.bfloat16)
    kept_q, kept_k, kept_v = lax.optimization_barrier((grad_tq, grad_tk, grad_tv))
    wide_q = kept_q.astype(jnp.float32)
    wide_k = kept_k.astype(jnp.float32)
    wide_v = kept_v.astype(jnp.float32)
    gain_terms = jnp.stack(
        [
            jnp.sum(wide_q * tile_normed.astype(jnp.float32), axis=(0, 1, 2, 3)),
            jnp.sum(wide_k * tile_warped.astype(jnp.float32), axis=(0, 1, 2, 3)),
            jnp.sum(wide_v * tile_warped.astype(jnp.float32), axis=(0, 1, 2, 3)),
        ]
    )
    direct, moved = (
        lax.all_to_all(
            (wide_q * gain_query).astype(jnp.bfloat16),
            "frame",
            split_axis=1,
            concat_axis=2,
            tiled=True,
        ).astype(jnp.float32),
        lax.all_to_all(
            (wide_k * gain_key + wide_v * gain_value).astype(jnp.bfloat16),
            "frame",
            split_axis=1,
            concat_axis=2,
            tiled=True,
        ).astype(jnp.float32),
    )
    grad_gains = lax.psum(gain_terms, ("clip", "frame"))
    onehot = (warp_lists[0, 0][:, None] == jnp.arange(tiles)[None, :]).astype(jnp.float32)
    grad_normed = direct + jnp.einsum(
        "js,xyjaf->xysaf", onehot, moved, precision=lax.Precision.HIGHEST
    )
    inner_sum = lax.psum(jnp.sum(grad_normed * spatial_f, axis=-1, keepdims=True), "mp")
    grad_spatial = (
        inverse * grad_normed - spatial_f * inverse**3 * (inner_sum / total_width)
    ).astype(jnp.bfloat16)
    back_q, back_k, back_v = attend_backward(
        to_heads(query_spatial),
        to_heads(key_spatial),
        to_heads(value_spatial),
        to_heads(grad_spatial),
        all_visible,
    )
    return (
        temporal_out,
        back_q.reshape(frame_shape).astype(jnp.bfloat16),
        back_k.reshape(frame_shape).astype(jnp.bfloat16),
        back_v.reshape(frame_shape).astype(jnp.bfloat16),
        grad_gains,
    )


def solution(mesh):
    return jax.shard_map(
        body,
        mesh=mesh,
        in_specs=(
            P("clip", "frame", None, None, "mp"),
            P("clip", "frame", None, None, "mp"),
            P("clip", "frame", None, None, "mp"),
            P(None, "mp"),
            P("clip", "frame", None),
            P("clip", None, "frame", None, "mp"),
        ),
        out_specs=(
            P("clip", None, "frame", None, "mp"),
            P("clip", "frame", None, None, "mp"),
            P("clip", "frame", None, None, "mp"),
            P("clip", "frame", None, None, "mp"),
            P(None, "mp"),
        ),
        check_vma=False,
    )
```

profile of v0, /device:TPU:0, one launch (start us, length us, event | category | flops | bytes accessed | tf_op | source)
XLA Modules:
  0.0 93.5 jit_solution(14472673728709017543)
XLA Ops:
  0.6 0.7 fusion.71
  1.3 1.1 %reshape.353 = bf16[80,5,128]{2,1,0:T(8,128)(2,1)S(1)} reshape(bf16[1,1,2,40,640]{4,3,2,1,0:T(8,128)(2,1)} %param.6) | data formatting | bytes 204800 | tf_op jit(solution)/shard_map/reshape | solution.py:68
  2.5 0.7 copy-done.1
  3.7 0.5 multiply_reduce_fusion.3
  4.3 8.4 %psum.21 = f32[1,1,2,40,1]{3,2,4,1,0:T(2,128)S(1)} all-reduce(f32[1,1,2,40,1]{3,2,4,1,0:T(2,128)S(1)} %broadcast_in_dim.46), channel_id=1, replica_groups=mesh['clip'=4,'frame'=2,'mp'=4] {'mp'}, use_global_device_ids=true, to_apply=%region_3.4 | all-reduce | flops 80 | bytes 640 | tf_op jit(solution)/shard_map/psum | solution.py:75
  12.8 0.7 fusion.67
  13.5 1.2 %gather_fusion = bf16[2,40,640]{2,1,0:T(8,128)(2,1)} fusion(bf16[2,40,640]{2,1,0:T(8,128)(2,1)S(1)} %get-tuple-element.34, s32[1024]{0:T(1024)S(1)} %pad_clamp_fusion), kind=kCustom, calls=%fused_computation | custom fusion | bytes 204808 | tf_op jit(solution)/shard_map/gather | solution.py:78
  14.7 3.5 %all-to-all-start = ((bf16[1,1,2,40,640]{4,3,1,0,2:T(8,128)(2,1)}), bf16[1,1,2,40,640]{4,3,1,0,2:T(8,128)(2,1)S(1)}, u32[]{:S(2)}, u32[]{:S(2)}) async-start(bf16[1,1,2,40,640]{4,3,1,0,2:T(8,128)(2,1)} %bitcast.6), calls=%async_computation | async-start | bytes 204800 | tf_op jit(solution)/shard_map/all_to_all | solution.py:81
  18.3 0.6 copy-done.3
  19.1 3.4 %all-to-all-done = bf16[1,1,2,40,640]{4,3,1,0,2:T(8,128)(2,1)S(1)} async-done(((bf16[1,1,2,40,640]{4,3,1,0,2:T(8,128)(2,1)}), bf16[1,1,2,40,640]{4,3,1,0,2:T(8,128)(2,1)S(1)}, u32[]{:S(2)}, u32[]{:S(2)}) %all-to-all-start) | async-done | bytes 102432 | tf_op jit(solution)/shard_map/all_to_all | solution.py:81
  22.5 3.3 %all-to-all-start.1 = ((bf16[1,1,2,40,640]{4,3,1,0,2:T(8,128)(2,1)}), bf16[1,1,2,40,640]{4,3,1,0,2:T(8,128)(2,1)S(1)}, u32[]{:S(2)}, u32[]{:S(2)}) async-start(bf16[1,1,2,40,640]{4,3,1,0,2:T(8,128)(2,1)} %get-tuple-element.33), calls=%async_computation.1 | async-start | bytes 204800 | tf_op jit(solution)/shard_map/all_to_all | solution.py:80
  25.9 4.2 %all-to-all-done.1 = bf16[1,1,2,40,640]{4,3,1,0,2:T(8,128)(2,1)S(1)} async-done(((bf16[1,1,2,40,640]{4,3,1,0,2:T(8,128)(2,1)}), bf16[1,1,2,40,640]{4,3,1,0,2:T(8,128)(2,1)S(1)}, u32[]{:S(2)}, u32[]{:S(2)}) %all-to-all-start.1) | async-done | bytes 102432 | tf_op jit(solution)/shard_map/all_to_all | solution.py:80
  32.6 0.7 fusion.34
  33.3 0.7 fusion.37
  34.0 3.3 %all-to-all-start.3 = ((bf16[1,2,1,40,640]{4,3,2,0,1:T(8,128)(2,1)}), bf16[1,2,1,40,640]{4,3,2,0,1:T(8,128)(2,1)S(1)}, u32[]{:S(2)}, u32[]{:S(2)}) async-start(bf16[1,2,1,40,640]{4,3,2,0,1:T(8,128)(2,1)} %get-tuple-element.35), calls=%async_computation.3 | async-start | bytes 204800 | tf_op jit(solution)/shard_map/all_to_all | solution.py:117
  37.4 0.8 reshape.356
  38.2 37.8 %psum.23 = f32[3,640]{1,0:T(4,128)} all-reduce(f32[3,640]{1,0:T(4,128)S(1)} %pad_maximum_fusion), channel_id=1, replica_groups=mesh['clip'=4,'frame'=2,'mp'=4] {'clip','frame'}, use_global_device_ids=true, to_apply=%region_13.14 | all-reduce | flops 1920 | bytes 15360 | tf_op jit(solution)/shard_map/psum | solution.py:125
  76.1 3.3 %all-to-all-start.2 = ((bf16[1,2,1,40,640]{4,3,2,0,1:T(8,128)(2,1)}), bf16[1,2,1,40,640]{4,3,2,0,1:T(8,128)(2,1)S(1)}, u32[]{:S(2)}, u32[]{:S(2)}) async-start(bf16[1,2,1,40,640]{4,3,2,0,1:T(8,128)(2,1)} %get-tuple-element.37), calls=%async_computation.2 | async-start | bytes 204800 | tf_op jit(solution)/shard_map/all_to_all | solution.py:110
  79.4 0.6 copy-done.4
  80.3 3.4 %all-to-all-done.2 = bf16[1,2,1,40,640]{4,3,2,0,1:T(8,128)(2,1)S(1)} async-done(((bf16[1,2,1,40,640]{4,3,2,0,1:T(8,128)(2,1)}), bf16[1,2,1,40,640]{4,3,2,0,1:T(8,128)(2,1)S(1)}, u32[]{:S(2)}, u32[]{:S(2)}) %all-to-all-start.2) | async-done | bytes 102432 | tf_op jit(solution)/shard_map/all_to_all | solution.py:110
  83.8 5.8 %psum.22 = f32[1,1,2,40,1]{3,2,4,1,0:T(2,128)S(1)} all-reduce(f32[1,1,2,40,1]{3,2,4,1,0:T(2,128)S(1)} %bitcast.101), channel_id=1, replica_groups=mesh['clip'=4,'frame'=2,'mp'=4] {'mp'}, use_global_device_ids=true, to_apply=%region_8.9 | all-reduce | flops 80 | bytes 640 | tf_op jit(solution)/shard_map/psum | solution.py:130
  91.1 0.8 convert_element_type.308
  91.9 0.8 convert_element_type.305
  92.8 0.8 convert_element_type.311
  (56 shorter events, 5.3 us)
Async XLA Ops:
  1.3 1.1 %copy-start = (bf16[1,1,2,40,640]{4,3,2,1,0:T(8,128)(2,1)S(1)}, bf16[1,1,2,40,640]{4,3,2,1,0:T(8,128)(2,1)}, u32[]{:S(2)}) copy-start(bf16[1,1,2,40,640]{4,3,2,1,0:T(8,128)(2,1)} %param.7) | copy-start | bytes 307204
  2.4 0.9 copy-start.1
  14.7 4.2 %copy-start.2 = (bf16[1,2,1,40,640]{4,3,2,1,0:T(8,128)(2,1)S(1)}, bf16[1,2,1,40,640]{4,3,2,1,0:T(8,128)(2,1)}, u32[]{:S(2)}) copy-start(bf16[1,2,1,40,640]{4,3,2,1,0:T(8,128)(2,1)} %param.11) | copy-start | bytes 307204
  14.7 7.8 %all-to-all-start = ((bf16[1,1,2,40,640]{4,3,1,0,2:T(8,128)(2,1)}), bf16[1,1,2,40,640]{4,3,1,0,2:T(8,128)(2,1)S(1)}, u32[]{:S(2)}, u32[]{:S(2)}) async-start(bf16[1,1,2,40,640]{4,3,1,0,2:T(8,128)(2,1)} %bitcast.6), calls=%async_computation | async-start | bytes 204800 | tf_op jit(solution)/shard_map/all_to_all | solution.py:81
  18.2 0.7 copy-start.3
  22.5 7.7 %all-to-all-start.1 = ((bf16[1,1,2,40,640]{4,3,1,0,2:T(8,128)(2,1)}), bf16[1,1,2,40,640]{4,3,1,0,2:T(8,128)(2,1)S(1)}, u32[]{:S(2)}, u32[]{:S(2)}) async-start(bf16[1,1,2,40,640]{4,3,1,0,2:T(8,128)(2,1)} %get-tuple-element.33), calls=%async_computation.1 | async-start | bytes 204800 | tf_op jit(solution)/shard_map/all_to_all | solution.py:80
  34.0 42.1 %all-to-all-start.3 = ((bf16[1,2,1,40,640]{4,3,2,0,1:T(8,128)(2,1)}), bf16[1,2,1,40,640]{4,3,2,0,1:T(8,128)(2,1)S(1)}, u32[]{:S(2)}, u32[]{:S(2)}) async-start(bf16[1,2,1,40,640]{4,3,2,0,1:T(8,128)(2,1)} %get-tuple-element.35), calls=%async_computation.3 | async-start | bytes 204800 | tf_op jit(solution)/shard_map/all_to_all | solution.py:117
  76.1 7.7 %all-to-all-start.2 = ((bf16[1,2,1,40,640]{4,3,2,0,1:T(8,128)(2,1)}), bf16[1,2,1,40,640]{4,3,2,0,1:T(8,128)(2,1)S(1)}, u32[]{:S(2)}, u32[]{:S(2)}) async-start(bf16[1,2,1,40,640]{4,3,2,0,1:T(8,128)(2,1)} %get-tuple-element.37), calls=%async_computation.2 | async-start | bytes 204800 | tf_op jit(solution)/shard_map/all_to_all | solution.py:110
  79.4 0.7 copy-start.4
where the time goes:
time: 94.2 us; the launch traced here: 93.5 us
  blocking collectives  52.1 us (55%)
  starting transfers between devices  13.5 us (14%)
  waiting for transfers between devices  11 us (12%)
  local copies, waits for them, and re-layouts  8.95 us (10%)
  other arithmetic  3.51 us (4%)
  matrix products  3.49 us (4%)
  between operations  0.98 us (1%)
    psum x1, blocking collectives, body(): grad_gains = lax.psum(gain_terms, ('clip', 'frame'))  37.8 us
    psum x1, blocking collectives, body(): lax.psum(jnp.sum(spatial_f * spatial_f, axis=-1, keepdims=True), 'mp')  8.36 us
    psum x1, blocking collectives, body(): lax.psum(jnp.sum(grad_normed * spatial_f, axis=-1, keepdims=True), 'mp')  5.85 us
    all_to_all x1, waiting for transfers between devices, body(): lax.all_to_all(normed, 'frame', split_axis=2, concat_axis=1, tiled=True)  4.24 us
    all_to_all x1, starting transfers between devices, body(): lax.all_to_all(warped, 'frame', split_axis=2, concat_axis=1, tiled=True)  3.47 us
    all_to_all x1, waiting for transfers between devices, body(): lax.all_to_all(warped, 'frame', split_axis=2, concat_axis=1, tiled=True)  3.42 us
    all_to_all x1, waiting for transfers between devices, body(): lax.all_to_all((wide_q * gain_query).astype(jnp.bfloat16), 'frame', split...  3.39 us
    all_to_all x1, starting transfers between devices, body(): lax.all_to_all((wide_q * gain_query).astype(jnp.bfloat16), 'frame', split...  3.34 us
  transfers between devices with their start and end apart: 4, of which 3 were waited for; matrix products, arithmetic and copies ran while one was open for 1% of the time, Pallas kernels for 0%

commit v1 on v0

v1 whole, which is shorter than its diff:
```python
import functools
import math

import jax
import jax.numpy as jnp
from jax import lax
from jax.experimental import pallas as pl
from jax.experimental.pallas import tpu as pltpu
from jax.sharding import PartitionSpec as P

HD = 128
MESH = pl.DeviceIdType.MESH
epsilon = 1e-06
F32 = jnp.float32
BF16 = jnp.bfloat16


def pad8(n):
    return (n + 7) // 8 * 8


def dot_nt(a, b):
    return lax.dot_general(a, b, (((1,), (1,)), ((), ())), preferred_element_type=F32)


def dot_nn(a, b):
    return lax.dot_general(a, b, (((1,), (0,)), ((), ())), preferred_element_type=F32)


def dot_tn(a, b):
    return lax.dot_general(a, b, (((0,), (0,)), ((), ())), preferred_element_type=F32)


def softmax(scores):
    top = jnp.max(scores, axis=-1, keepdims=True)
    expon = jnp.exp(scores - top)
    return expon / jnp.sum(expon, axis=-1, keepdims=True)


def kernel(
    dims,
    q_ref,
    k_ref,
    v_ref,
    gains_ref,
    warp_ref,
    cot_ref,
    tout_ref,
    gq_ref,
    gk_ref,
    gv_ref,
    gg_ref,
    p_sc,
    sp_sc,
    table_sc,
    a_send,
    a_recv,
    sq_send,
    sq_recv,
    b_send,
    b_recv,
    in_send,
    in_recv,
    g_send,
    g_recv,
    a_ss,
    a_rs,
    sq_ss,
    sq_rs,
    b_ss,
    b_rs,
    in_ss,
    in_rs,
    g_ss,
    g_rs,
):
    clips, frames, mps, tiles, tt, heads = dims
    total_width = float(heads * HD * mps)
    scale = 1.0 / math.sqrt(HD)
    c = lax.axis_index("clip")
    f = lax.axis_index("frame")
    m = lax.axis_index("mp")

    def at(index, step, size):
        return lax.rem(index + step, size) if step else index

    group = [(df, dm) for df in range(frames) for dm in range(mps) if (df, dm) != (0, 0)]
    wide = [(dc, df) for dc in range(clips) for df in range(frames) if (dc, df) != (0, 0)]

    def in_group(df, dm):
        return {"frame": at(f, df, frames), "mp": at(m, dm, mps)}

    def in_wide(dc, df):
        return {"clip": at(c, dc, clips), "frame": at(f, df, frames)}

    barrier = pltpu.get_barrier_semaphore()
    peers = [in_group(*step) for step in group]
    peers += [in_wide(dc, df) for dc, df in wide if dc]
    for peer in peers:
        pl.semaphore_signal(barrier, inc=1, device_id=peer, device_id_type=MESH)

    def head_cols(h):
        if isinstance(h, int):
            return slice(h * HD, (h + 1) * HD)
        return pl.ds(pl.multiple_of(h * HD, HD), HD)

    def each_head(fn, carry):
        if tiles * tt <= 128:
            for h in range(heads):
                carry = fn(h, carry)
            return carry
        return lax.fori_loop(0, heads, fn, carry)

    def send(src, dst, send_sem, recv_sem, peer):
        copy = pltpu.make_async_remote_copy(
            src_ref=src,
            dst_ref=dst,
            send_sem=send_sem,
            recv_sem=recv_sem,
            device_id=peer,
            device_id_type=MESH,
        )
        copy.start()
        return copy

    diagonal = lax.broadcasted_iota(jnp.int32, (tt, HD), 0) == lax.broadcasted_iota(
        jnp.int32, (tt, HD), 1
    )

    def to_row(column):
        return jnp.sum(jnp.where(diagonal, column, 0.0), axis=0, keepdims=True)

    def to_column(row):
        return jnp.sum(jnp.where(diagonal, row, 0.0), axis=1, keepdims=True)

    def spatial_head(h, squares):
        cols = head_cols(h)
        weights = softmax(dot_nt(q_ref[:, cols], k_ref[:, cols]) * scale)
        p_sc[h] = weights
        out = dot_nn(weights.astype(BF16), v_ref[:, cols]).astype(BF16).astype(F32)
        sp_sc[:, cols] = out
        return squares + out * out

    squares = each_head(spatial_head, jnp.zeros((tiles * tt, HD), F32))
    square_sum = jnp.sum(squares, axis=1, keepdims=True)
    for s in range(tiles):
        table_sc[pl.ds(s, 1), :] = to_row(square_sum[s * tt : (s + 1) * tt])

    def reads(j, s):
        return jnp.where(jnp.full((1, HD), warp_ref[j], jnp.int32) == s, 1.0, 0.0)

    def tile_pair(ref, j):
        picks = [reads(j, s) for s in range(tiles)]

        def one_head(h, carry):
            cols = head_cols(h)
            own = sp_sc[pl.ds(pl.multiple_of(j * tt, 8), tt), cols]
            source = picks[0] * sp_sc[0:tt, cols]
            for s in range(1, tiles):
                source = source + picks[s] * sp_sc[s * tt : (s + 1) * tt, cols]
            ref[:, cols] = jnp.concatenate([own, source], axis=0).astype(BF16)
            return carry

        each_head(one_head, 0)

    def square_rows(ref, j):
        source = reads(j, 0) * table_sc[0:1, :]
        for s in range(1, tiles):
            source = source + reads(j, s) * table_sc[s : s + 1, :]
        ref[0:1, :] = table_sc[pl.ds(j, 1), :]
        ref[1:2, :] = source
        ref[2 : 2 + tiles, :] = table_sc[0:tiles, :]

    pl.semaphore_wait(barrier, len(peers))

    flying = []
    for df in range(1, frames):
        j = at(f, df, frames)
        tile_pair(a_send.at[df], j)
        flying.append(send(a_send.at[df], a_recv.at[f], a_ss.at[df], a_rs.at[df], {"frame": j}))
    for df in range(frames):
        square_rows(sq_send.at[df], at(f, df, frames))
    for df, dm in group:
        flying.append(
            send(
                sq_send.at[df],
                sq_recv.at[f, m],
                sq_ss.at[df, dm],
                sq_rs.at[df, dm],
                in_group(df, dm),
            )
        )
    tile_pair(a_recv.at[f], f)
    sq_recv[f, m] = sq_send[0]
    for copy in flying:
        copy.wait()

    inverse_rows = []
    for t in range(frames):
        total = sq_recv[t, 0]
        for other in range(1, mps):
            total = total + sq_recv[t, other]
        inverse_rows.append(lax.rsqrt(total / total_width + epsilon))
    inverse_own = jnp.concatenate([to_column(rows[0:1]) for rows in inverse_rows], axis=0)
    inverse_source = jnp.concatenate([to_column(rows[1:2]) for rows in inverse_rows], axis=0)
    count = frames * tt
    frame_q = lax.broadcasted_iota(jnp.int32, (count, count), 0) // tt
    frame_k = lax.broadcasted_iota(jnp.int32, (count, count), 1) // tt
    causal = frame_q >= frame_k

    def temporal_head(h, carry):
        dot_own, dot_source = carry
        cols = head_cols(h)
        blocks = [a_recv[t, :, cols].astype(F32) for t in range(frames)]
        own = jnp.concatenate([block[:tt] for block in blocks], axis=0)
        source = jnp.concatenate([block[tt:] for block in blocks], axis=0)
        normed = (own * inverse_own).astype(BF16).astype(F32)
        warped = (source * inverse_source).astype(BF16).astype(F32)
        gain_q = gains_ref[0:1, cols]
        gain_k = gains_ref[1:2, cols]
        gain_v = gains_ref[2:3, cols]
        tq = (normed * gain_q).astype(BF16)
        tk = (warped * gain_k).astype(BF16)
        tv = (warped * gain_v).astype(BF16)
        weights = softmax(jnp.where(causal, dot_nt(tq, tk) * scale, -1e30))
        rounded = weights.astype(BF16)
        tout_ref[:, cols] = dot_nn(rounded, tv).astype(BF16)
        upstream = cot_ref[:, cols]
        grad_weights = dot_nt(upstream, tv)
        inner = jnp.sum(weights * grad_weights, axis=-1, keepdims=True)
        grad_scores = (weights * (grad_weights - inner) * scale).astype(BF16)
        dq = dot_nn(grad_scores, tk).astype(BF16).astype(F32)
        dk = dot_tn(grad_scores, tq).astype(BF16).astype(F32)
        dv = dot_tn(rounded, upstream).astype(BF16).astype(F32)
        direct = (dq * gain_q).astype(BF16).astype(F32)
        moved = (dk * gain_k + dv * gain_v).astype(BF16).astype(F32)
        for t in range(frames):
            rows = slice(t * tt, (t + 1) * tt)
            b_send[t, :, cols] = jnp.concatenate([direct[rows], moved[rows]], axis=0).astype(BF16)
        g_send[pl.ds(h, 1), :] = jnp.sum(dq * normed, axis=0, keepdims=True)
        g_send[pl.ds(heads + h, 1), :] = jnp.sum(dk * warped, axis=0, keepdims=True)
        g_send[pl.ds(2 * heads + h, 1), :] = jnp.sum(dv * warped, axis=0, keepdims=True)
        return dot_own + direct * own, dot_source + moved * source

    zero = jnp.zeros((count, HD), F32)
    dot_own, dot_source = each_head(temporal_head, (zero, zero))

    flying = []
    for df in range(1, frames):
        t = at(f, df, frames)
        flying.append(send(b_send.at[t], b_recv.at[f], b_ss.at[df], b_rs.at[df], {"frame": t}))
    dot_own = jnp.sum(dot_own, axis=1, keepdims=True)
    dot_source = jnp.sum(dot_source, axis=1, keepdims=True)
    for t in range(frames):
        rows = slice(t * tt, (t + 1) * tt)
        in_send[t, 0:1, :] = to_row(dot_own[rows])
        in_send[t, 1:2, :] = to_row(dot_source[rows])
    for df, dm in group:
        flying.append(
            send(
                in_send.at[at(f, df, frames)],
                in_recv.at[f, m],
                in_ss.at[df, dm],
                in_rs.at[df, dm],
                in_group(df, dm),
            )
        )
    sums = []
    for dc, df in wide:
        sums.append(
            send(g_send, g_recv.at[c, f], g_ss.at[dc, df], g_rs.at[dc, df], in_wide(dc, df))
        )
    b_recv[f] = b_send[f]
    in_recv[f, m] = in_send[f]
    g_recv[c, f] = g_send[...]
    for copy in flying:
        copy.wait()

    total = sq_recv[f, 0]
    for other in range(1, mps):
        total = total + sq_recv[f, other]
    inverse_table = lax.rsqrt(total / total_width + epsilon)
    inner_rows = []
    for j in range(tiles):
        rows = in_recv[j, 0]
        for other in range(1, mps):
            rows = rows + in_recv[j, other]
        inner_rows.append(rows)
    factors = []
    for s in range(tiles):
        row = inner_rows[s][0:1]
        for j in range(tiles):
            row = row + reads(j, s) * inner_rows[j][1:2]
        inverse = to_column(inverse_table[2 + s : 3 + s])
        inner = to_column(row)
        factors.append((inverse, inverse * inverse * inverse * (inner / total_width)))

    def backward_head(h, carry):
        cols = head_cols(h)
        blocks = [b_recv[j, :, cols].astype(F32) for j in range(tiles)]
        parts = []
        for s in range(tiles):
            grad = blocks[s][:tt]
            for j in range(tiles):
                grad = grad + reads(j, s) * blocks[j][tt:]
            inverse, factor = factors[s]
            parts.append(inverse * grad - sp_sc[s * tt : (s + 1) * tt, cols] * factor)
        upstream = jnp.concatenate(parts, axis=0).astype(BF16)
        weights = p_sc[h]
        grad_weights = dot_nt(upstream, v_ref[:, cols])
        inner = jnp.sum(weights * grad_weights, axis=-1, keepdims=True)
        grad_scores = (weights * (grad_weights - inner) * scale).astype(BF16)
        gq_ref[:, cols] = dot_nn(grad_scores, k_ref[:, cols]).astype(BF16)
        gk_ref[:, cols] = dot_tn(grad_scores, q_ref[:, cols]).astype(BF16)
        gv_ref[:, cols] = dot_tn(weights.astype(BF16), upstream).astype(BF16)
        return carry

    each_head(backward_head, 0)

    for copy in sums:
        copy.wait()
    total = None
    for other in range(clips):
        for t in range(frames):
            total = g_recv[other, t] if total is None else total + g_recv[other, t]
    for g in range(3):
        for h in range(heads):
            row = g * heads + h
            gg_ref[g : g + 1, h * HD : (h + 1) * HD] = total[row : row + 1]


def body(sizes, query, key, value, gains, warp_lists, cotangent):
    clips, frames, mps = sizes
    tiles, tt, width = query.shape[2:]
    heads = width // HD
    count = tiles * tt
    dims = (clips, frames, mps, tiles, tt, heads)
    vmem = pl.BlockSpec(memory_space=pltpu.VMEM)
    table = pad8(tiles + 2)
    gain_rows = pad8(3 * heads)
    dma = pltpu.SemaphoreType.DMA
    outs = pl.pallas_call(
        functools.partial(kernel, dims),
        out_shape=(
            jax.ShapeDtypeStruct((frames * tt, width), BF16),
            jax.ShapeDtypeStruct((count, width), BF16),
            jax.ShapeDtypeStruct((count, width), BF16),
            jax.ShapeDtypeStruct((count, width), BF16),
            jax.ShapeDtypeStruct((3, width), F32),
        ),
        in_specs=[vmem, vmem, vmem, vmem, pl.BlockSpec(memory_space=pltpu.SMEM), vmem],
        out_specs=(vmem,) * 5,
        scratch_shapes=[
            pltpu.VMEM((heads, count, count), F32),
            pltpu.VMEM((count, width), F32),
            pltpu.VMEM((pad8(tiles), HD), F32),
            pltpu.VMEM((frames, 2 * tt, width), BF16),
            pltpu.VMEM((frames, 2 * tt, width), BF16),
            pltpu.VMEM((frames, table, HD), F32),
            pltpu.VMEM((frames, mps, table, HD), F32),
            pltpu.VMEM((frames, 2 * tt, width), BF16),
            pltpu.VMEM((frames, 2 * tt, width), BF16),
            pltpu.VMEM((frames, 8, HD), F32),
            pltpu.VMEM((frames, mps, 8, HD), F32),
            pltpu.VMEM((gain_rows, HD), F32),
            pltpu.VMEM((clips, frames, gain_rows, HD), F32),
            dma((frames,)),
            dma((frames,)),
            dma((frames, mps)),
            dma((frames, mps)),
            dma((frames,)),
            dma((frames,)),
            dma((frames, mps)),
            dma((frames, mps)),
            dma((clips, frames)),
            dma((clips, frames)),
        ],
        compiler_params=pltpu.CompilerParams(
            collective_id=0, has_side_effects=True, vmem_limit_bytes=56 * 2**20
        ),
    )(
        query.reshape(count, width),
        key.reshape(count, width),
        value.reshape(count, width),
        gains,
        warp_lists.reshape(tiles),
        cotangent.reshape(frames * tt, width),
    )
    temporal, back_q, back_k, back_v, grad_gains = outs
    return (
        temporal.reshape(cotangent.shape),
        back_q.reshape(query.shape),
        back_k.reshape(query.shape),
        back_v.reshape(query.shape),
        grad_gains,
    )


def solution(mesh):
    sizes = (mesh.shape["clip"], mesh.shape["frame"], mesh.shape["mp"])
    return jax.shard_map(
        functools.partial(body, sizes),
        mesh=mesh,
        in_specs=(
            P("clip", "frame", None, None, "mp"),
            P("clip", "frame", None, None, "mp"),
            P("clip", "frame", None, None, "mp"),
            P(None, "mp"),
            P("clip", "frame", None),
            P("clip", None, "frame", None, "mp"),
        ),
        out_specs=(
            P("clip", None, "frame", None, "mp"),
            P("clip", "frame", None, None, "mp"),
            P("clip", "frame", None, None, "mp"),
            P("clip", "frame", None, None, "mp"),
            P(None, "mp"),
        ),
        check_vma=False,
    )
```

time: 94.2 us -> 28.3 us (0.30)
  blocking collectives: 52.1 us -> 0 us
  Pallas kernels: 0 us -> 22.6 us
  starting transfers between devices: 13.5 us -> 0 us
  waiting for transfers between devices: 11 us -> 0 us
  local copies, waits for them, and re-layouts: 8.95 us -> 4.75 us
  other arithmetic: 3.51 us -> 0 us
  matrix products: 3.49 us -> 0 us
    psum x3 -> x0, blocking collectives: 52.1 us -> none  [the longest x1 37.8 us: body(): grad_gains = lax.psum(gain_terms, ('clip', 'frame'))]
    pallas_call x0 -> x1, Pallas kernels: none -> 22.6 us  [body(): pl.pallas_call(functools.partial(kernel, dims), out_shape=(jax.ShapeDtype...]
    all_to_all x4 -> x0, starting transfers between devices: 13.5 us -> none  [the longest x1 3.47 us: body(): lax.all_to_all(warped, 'frame', split_axis=2, concat_axis=1, tiled=True)]
    all_to_all x4 -> x0, waiting for transfers between devices: 11 us -> none  [the longest x1 4.24 us: body(): lax.all_to_all(normed, 'frame', split_axis=2, concat_axis=1, tiled=True)]
    convert_element_type x17 -> x0, local copies, waits for them, and re-layouts: 3.26 us -> none  [the longest x2 0.82 us: body(): back_k.reshape(frame_shape).astype(jnp.bfloat16)]
    dot_general x12 -> x0, matrix products: 3.24 us -> none  [the longest x2 0.78 us: attend_forward(): jnp.einsum('hqk,khd->qhd', rounded, value_rows, preferred_element_type=jn...]
    unnamed x10 -> x13, local copies, waits for them, and re-layouts: 2.01 us -> 4.75 us
    reshape x6 -> x0, local copies, waits for them, and re-layouts: 2.37 us -> none  [the longest x5 1.59 us: to_heads(): return array.reshape(-1, heads_here, HD)]
  transfers between devices with their start and end apart: 4 -> 0, of which waited for: 3 -> 0; matrix products, arithmetic and copies ran while one was open for 1% -> 0% of each run, Pallas kernels for 0% -> 0%
where the time goes in v1:
time: 28.3 us; the launch traced here: 28 us
  Pallas kernels  22.6 us (80%)
  local copies, waits for them, and re-layouts  4.75 us (17%)
  between operations  0.65 us (2%)
    pallas_call x1, Pallas kernels, body(): pl.pallas_call(functools.partial(kernel, dims), out_shape=(jax.ShapeDtype...  22.6 us
    unnamed x13, local copies, waits for them, and re-layouts  4.75 us

profile of v1, /device:TPU:0, one launch (start us, length us, event | category | flops | bytes accessed | tf_op | source)
XLA Modules:
  0.0 28.0 jit_solution(3608257692677331049)
XLA Ops:
  0.6 22.6 %shard_map.101 = (bf16[80,640]{1,0:T(8,128)(2,1)}, bf16[80,640]{1,0:T(8,128)(2,1)}, bf16[80,640]{1,0:T(8,128)(2,1)}, bf16[80,640]{1,0:T(8,128)(2,1)}, f32[3,640]{1,0:T(4,128)}) custom-call(bf16[80,640]{1,0:T(8,128)(2,1)} %bitcast.11, bf16[80,640]{1,0:T(8,128)(2,1)} %bitcast.12, bf16[80,640]{1,0:T(8,128)(2,1)} %bitcast.13, f32[3,640]{1,0:T(4,128)} %gains_ref.1, ...), custom_call_target="tpu_custom_call" | custom-call | tf_op jit(solution)/shard_map/pallas_call | solution.py:342
  23.2 0.0 copy-start.2
  23.2 1.6 %copy.17 = bf16[1,2,1,40,640]{4,3,2,1,0:T(8,128)(2,1)} copy(bf16[1,2,1,40,640]{4,3,2,1,0:T(8,128)(2,1)} %bitcast.18) | data formatting | bytes 204800
  24.8 0.0 copy-done.2
  24.8 0.0 copy-start.1
  24.8 0.6 %copy.18 = bf16[1,1,2,40,640]{4,3,2,1,0:T(8,128)(2,1)} copy(bf16[1,1,2,40,640]{4,3,2,1,0:T(8,128)(2,1)S(1)} %bitcast.17) | data formatting | bytes 204800
  25.5 0.3 %copy-done.1 = bf16[80,640]{1,0:T(8,128)(2,1)S(1)} copy-done((bf16[80,640]{1,0:T(8,128)(2,1)S(1)}, bf16[80,640]{1,0:T(8,128)(2,1)}, u32[]{:S(2)}) %copy-start.1) | copy-done | bytes 102424
  25.7 0.0 copy-start
  25.7 0.6 %copy.19 = bf16[1,1,2,40,640]{4,3,2,1,0:T(8,128)(2,1)} copy(bf16[1,1,2,40,640]{4,3,2,1,0:T(8,128)(2,1)S(1)} %bitcast.16) | data formatting | bytes 204800
  26.4 0.3 %copy-done = bf16[80,640]{1,0:T(8,128)(2,1)S(1)} copy-done((bf16[80,640]{1,0:T(8,128)(2,1)S(1)}, bf16[80,640]{1,0:T(8,128)(2,1)}, u32[]{:S(2)}) %copy-start) | copy-done | bytes 102424
  26.7 0.0 copy-start.3
  26.7 0.6 %copy.20 = bf16[1,1,2,40,640]{4,3,2,1,0:T(8,128)(2,1)} copy(bf16[1,1,2,40,640]{4,3,2,1,0:T(8,128)(2,1)S(1)} %bitcast.15) | data formatting | bytes 204800
  27.3 0.1 copy-done.3
  27.4 0.6 %copy.21 = f32[3,640]{1,0:T(4,128)} copy(f32[3,640]{1,0:T(4,128)S(1)} %copy-done.3) | data formatting | bytes 15360
Async XLA Ops:
  23.2 1.6 %copy-start.2 = (bf16[80,640]{1,0:T(8,128)(2,1)S(1)}, bf16[80,640]{1,0:T(8,128)(2,1)}, u32[]{:S(2)}) copy-start(bf16[80,640]{1,0:T(8,128)(2,1)} %get-tuple-element.11) | copy-start | bytes 307204
  24.8 0.9 %copy-start.1 = (bf16[80,640]{1,0:T(8,128)(2,1)S(1)}, bf16[80,640]{1,0:T(8,128)(2,1)}, u32[]{:S(2)}) copy-start(bf16[80,640]{1,0:T(8,128)(2,1)} %get-tuple-element.12) | copy-start | bytes 307204
  25.7 0.9 %copy-start = (bf16[80,640]{1,0:T(8,128)(2,1)S(1)}, bf16[80,640]{1,0:T(8,128)(2,1)}, u32[]{:S(2)}) copy-start(bf16[80,640]{1,0:T(8,128)(2,1)} %get-tuple-element.13) | copy-start | bytes 307204
  26.7 0.7 %copy-start.3 = (f32[3,640]{1,0:T(4,128)S(1)}, f32[3,640]{1,0:T(4,128)}, u32[]{:S(2)}) copy-start(f32[3,640]{1,0:T(4,128)} %get-tuple-element.29) | copy-start | bytes 23044

commit v2 on v1

--- a/solution.py
+++ b/solution.py
@@ -329,6 +329,15 @@
             gg_ref[g : g + 1, h * HD : (h + 1) * HD] = total[row : row + 1]
 
 
+def write_out(*refs):
+    sems = refs[10]
+    copies = [pltpu.make_async_copy(refs[i], refs[5 + i], sems.at[i]) for i in range(5)]
+    for copy in copies:
+        copy.start()
+    for copy in copies:
+        copy.wait()
+
+
 def body(sizes, query, key, value, gains, warp_lists, cotangent):
     clips, frames, mps = sizes
     tiles, tt, width = query.shape[2:]
@@ -339,15 +348,10 @@
     table = pad8(tiles + 2)
     gain_rows = pad8(3 * heads)
     dma = pltpu.SemaphoreType.DMA
+    results = [((frames * tt, width), BF16)] + [((count, width), BF16)] * 3 + [((3, width), F32)]
     outs = pl.pallas_call(
         functools.partial(kernel, dims),
-        out_shape=(
-            jax.ShapeDtypeStruct((frames * tt, width), BF16),
-            jax.ShapeDtypeStruct((count, width), BF16),
-            jax.ShapeDtypeStruct((count, width), BF16),
-            jax.ShapeDtypeStruct((count, width), BF16),
-            jax.ShapeDtypeStruct((3, width), F32),
-        ),
+        out_shape=tuple(pltpu.VMEM(shape, kind) for shape, kind in results),
         in_specs=[vmem, vmem, vmem, vmem, pl.BlockSpec(memory_space=pltpu.SMEM), vmem],
         out_specs=(vmem,) * 5,
         scratch_shapes=[
@@ -386,6 +390,13 @@
         warp_lists.reshape(tiles),
         cotangent.reshape(frames * tt, width),
     )
+    outs = pl.pallas_call(
+        write_out,
+        out_shape=tuple(jax.ShapeDtypeStruct(shape, kind) for shape, kind in results),
+        in_specs=[vmem] * 5,
+        out_specs=(pl.BlockSpec(memory_space=pl.ANY),) * 5,
+        scratch_shapes=[dma((5,))],
+    )(*(pltpu.with_memory_space_constraint(out, pltpu.VMEM) for out in outs))
     temporal, back_q, back_k, back_v, grad_gains = outs
     return (
         temporal.reshape(cotangent.shape),

time: 28.3 us -> 23.4 us (0.83)
  local copies, waits for them, and re-layouts: 4.75 us -> 0 us
    unnamed x13 -> x0, local copies, waits for them, and re-layouts: 4.75 us -> none
    pallas_call x1 -> x2, Pallas kernels: 22.6 us -> 22.6 us  [the longest x1 21.8 us: body(): pl.pallas_call(functools.partial(kernel, dims), out_shape=tuple((pltpu.VM...]
where the time goes in v2:
time: 23.4 us; the launch traced here: 23.3 us
  Pallas kernels  22.6 us (97%)
  between operations  0.64 us (3%)
    pallas_call x1, Pallas kernels, body(): pl.pallas_call(functools.partial(kernel, dims), out_shape=tuple((pltpu.VM...  21.8 us
    pallas_call x1, Pallas kernels, body(): pl.pallas_call(write_out, out_shape=tuple((jax.ShapeDtypeStruct(shape, ki...  0.79 us

profile of v2, /device:TPU:0, one launch (start us, length us, event | category | flops | bytes accessed | tf_op | source)
XLA Modules:
  0.0 23.3 jit_solution(14931037568319818748)
XLA Ops:
  0.6 21.8 %shard_map.101 = (bf16[80,640]{1,0:T(8,128)(2,1)S(1)}, bf16[80,640]{1,0:T(8,128)(2,1)S(1)}, bf16[80,640]{1,0:T(8,128)(2,1)S(1)}, bf16[80,640]{1,0:T(8,128)(2,1)S(1)}, f32[3,640]{1,0:T(4,128)S(1)}) custom-call(bf16[80,640]{1,0:T(8,128)(2,1)} %bitcast.11, bf16[80,640]{1,0:T(8,128)(2,1)} %bitcast.12, bf16[80,640]{1,0:T(8,128)(2,1)} %bitcast.13, ...), custom_call_target="tpu_custom_call" | custom-call | tf_op jit(solution)/shard_map/pallas_call | solution.py:352
  22.5 0.8 %shard_map.102 = (bf16[80,640]{1,0:T(8,128)(2,1)}, bf16[80,640]{1,0:T(8,128)(2,1)}, bf16[80,640]{1,0:T(8,128)(2,1)}, bf16[80,640]{1,0:T(8,128)(2,1)}, f32[3,640]{1,0:T(4,128)}) custom-call(bf16[80,640]{1,0:T(8,128)(2,1)S(1)} %get-tuple-element.15.refs_0_, bf16[80,640]{1,0:T(8,128)(2,1)S(1)} %get-tuple-element.16.refs_1_, ...), custom_call_target="tpu_custom_call" | custom-call | tf_op jit(solution)/shard_map/pallas_call | solution.py:393

commit v3 on v2

--- a/solution.py
+++ b/solution.py
@@ -19,6 +19,11 @@
     return (n + 7) // 8 * 8
 
 
+def cuts(heads):
+    middle = (heads + 1) // 2
+    return [(0, middle), (middle, heads)]
+
+
 def dot_nt(a, b):
     return lax.dot_general(a, b, (((1,), (1,)), ((), ())), preferred_element_type=F32)
 
@@ -31,10 +36,10 @@
     return lax.dot_general(a, b, (((0,), (0,)), ((), ())), preferred_element_type=F32)
 
 
-def softmax(scores):
-    top = jnp.max(scores, axis=-1, keepdims=True)
-    expon = jnp.exp(scores - top)
-    return expon / jnp.sum(expon, axis=-1, keepdims=True)
+def softmax(scores, scale):
+    top = jnp.max(scores, axis=0, keepdims=True)
+    expon = jnp.exp((scores - top) * scale)
+    return expon * (1.0 / jnp.sum(expon, axis=0, keepdims=True))
 
 
 def kernel(
@@ -84,6 +89,7 @@
     def at(index, step, size):
         return lax.rem(index + step, size) if step else index
 
+    groups = cuts(heads)
     group = [(df, dm) for df in range(frames) for dm in range(mps) if (df, dm) != (0, 0)]
     wide = [(dc, df) for dc in range(clips) for df in range(frames) if (dc, df) != (0, 0)]
 
@@ -104,12 +110,12 @@
             return slice(h * HD, (h + 1) * HD)
         return pl.ds(pl.multiple_of(h * HD, HD), HD)
 
-    def each_head(fn, carry):
+    def each_head(fn, carry, low=0, high=heads):
         if tiles * tt <= 128:
-            for h in range(heads):
+            for h in range(low, high):
                 carry = fn(h, carry)
             return carry
-        return lax.fori_loop(0, heads, fn, carry)
+        return lax.fori_loop(low, high, fn, carry)
 
     def send(src, dst, send_sem, recv_sem, peer):
         copy = pltpu.make_async_remote_copy(
@@ -135,21 +141,16 @@
 
     def spatial_head(h, squares):
         cols = head_cols(h)
-        weights = softmax(dot_nt(q_ref[:, cols], k_ref[:, cols]) * scale)
+        weights = softmax(dot_nt(k_ref[:, cols], q_ref[:, cols]), scale)
         p_sc[h] = weights
-        out = dot_nn(weights.astype(BF16), v_ref[:, cols]).astype(BF16).astype(F32)
+        out = dot_tn(weights.astype(BF16), v_ref[:, cols]).astype(BF16).astype(F32)
         sp_sc[:, cols] = out
         return squares + out * out
 
-    squares = each_head(spatial_head, jnp.zeros((tiles * tt, HD), F32))
-    square_sum = jnp.sum(squares, axis=1, keepdims=True)
-    for s in range(tiles):
-        table_sc[pl.ds(s, 1), :] = to_row(square_sum[s * tt : (s + 1) * tt])
-
     def reads(j, s):
         return jnp.where(jnp.full((1, HD), warp_ref[j], jnp.int32) == s, 1.0, 0.0)
 
-    def tile_pair(ref, j):
+    def tile_pair(ref, j, low, high):
         picks = [reads(j, s) for s in range(tiles)]
 
         def one_head(h, carry):
@@ -158,10 +159,10 @@
             source = picks[0] * sp_sc[0:tt, cols]
             for s in range(1, tiles):
                 source = source + picks[s] * sp_sc[s * tt : (s + 1) * tt, cols]
-            ref[:, cols] = jnp.concatenate([own, source], axis=0).astype(BF16)
+            ref[h] = jnp.concatenate([own, source], axis=0).astype(BF16)
             return carry
 
-        each_head(one_head, 0)
+        each_head(one_head, 0, low, high)
 
     def square_rows(ref, j):
         source = reads(j, 0) * table_sc[0:1, :]
@@ -171,16 +172,30 @@
         ref[1:2, :] = source
         ref[2 : 2 + tiles, :] = table_sc[0:tiles, :]
 
-    pl.semaphore_wait(barrier, len(peers))
-
     flying = []
-    for df in range(1, frames):
-        j = at(f, df, frames)
-        tile_pair(a_send.at[df], j)
-        flying.append(send(a_send.at[df], a_recv.at[f], a_ss.at[df], a_rs.at[df], {"frame": j}))
+    squares = jnp.zeros((tiles * tt, HD), F32)
+    for part, (low, high) in enumerate(groups):
+        squares = each_head(spatial_head, squares, low, high)
+        if part == 0:
+            pl.semaphore_wait(barrier, len(peers))
+        for df in range(1, frames):
+            j = at(f, df, frames)
+            tile_pair(a_send.at[df], j, low, high)
+            flying.append(
+                send(
+                    a_send.at[df, low:high],
+                    a_recv.at[f, low:high],
+                    a_ss.at[df, part],
+                    a_rs.at[df, part],
+                    {"frame": j},
+                )
+            )
+    square_sum = jnp.sum(squares, axis=1, keepdims=True)
+    for s in range(tiles):
+        table_sc[pl.ds(s, 1), :] = to_row(square_sum[s * tt : (s + 1) * tt])
     for df in range(frames):
         square_rows(sq_send.at[df], at(f, df, frames))
-    for df, dm in group:
+    for df, dm in reversed(group):
         flying.append(
             send(
                 sq_send.at[df],
@@ -190,10 +205,11 @@
                 in_group(df, dm),
             )
         )
-    tile_pair(a_recv.at[f], f)
+    tile_pair(a_recv.at[f], f, 0, heads)
     sq_recv[f, m] = sq_send[0]
     for copy in flying:
-        copy.wait()
+        copy.wait_recv()
+    sent = flying
 
     inverse_rows = []
     for t in range(frames):
@@ -204,14 +220,14 @@
     inverse_own = jnp.concatenate([to_column(rows[0:1]) for rows in inverse_rows], axis=0)
     inverse_source = jnp.concatenate([to_column(rows[1:2]) for rows in inverse_rows], axis=0)
     count = frames * tt
-    frame_q = lax.broadcasted_iota(jnp.int32, (count, count), 0) // tt
-    frame_k = lax.broadcasted_iota(jnp.int32, (count, count), 1) // tt
+    frame_k = lax.broadcasted_iota(jnp.int32, (count, count), 0) // tt
+    frame_q = lax.broadcasted_iota(jnp.int32, (count, count), 1) // tt
     causal = frame_q >= frame_k
 
     def temporal_head(h, carry):
         dot_own, dot_source = carry
         cols = head_cols(h)
-        blocks = [a_recv[t, :, cols].astype(F32) for t in range(frames)]
+        blocks = [a_recv[t, h].astype(F32) for t in range(frames)]
         own = jnp.concatenate([block[:tt] for block in blocks], axis=0)
         source = jnp.concatenate([block[tt:] for block in blocks], axis=0)
         normed = (own * inverse_own).astype(BF16).astype(F32)
@@ -222,33 +238,43 @@
         tq = (normed * gain_q).astype(BF16)
         tk = (warped * gain_k).astype(BF16)
         tv = (warped * gain_v).astype(BF16)
-        weights = softmax(jnp.where(causal, dot_nt(tq, tk) * scale, -1e30))
+        weights = softmax(jnp.where(causal, dot_nt(tk, tq), -1e30), scale)
         rounded = weights.astype(BF16)
-        tout_ref[:, cols] = dot_nn(rounded, tv).astype(BF16)
+        tout_ref[:, cols] = dot_tn(rounded, tv).astype(BF16)
         upstream = cot_ref[:, cols]
-        grad_weights = dot_nt(upstream, tv)
-        inner = jnp.sum(weights * grad_weights, axis=-1, keepdims=True)
+        grad_weights = dot_nt(tv, upstream)
+        inner = jnp.sum(weights * grad_weights, axis=0, keepdims=True)
         grad_scores = (weights * (grad_weights - inner) * scale).astype(BF16)
-        dq = dot_nn(grad_scores, tk).astype(BF16).astype(F32)
-        dk = dot_tn(grad_scores, tq).astype(BF16).astype(F32)
-        dv = dot_tn(rounded, upstream).astype(BF16).astype(F32)
+        dq = dot_tn(grad_scores, tk).astype(BF16).astype(F32)
+        dk = dot_nn(grad_scores, tq).astype(BF16).astype(F32)
+        dv = dot_nn(rounded, upstream).astype(BF16).astype(F32)
         direct = (dq * gain_q).astype(BF16).astype(F32)
         moved = (dk * gain_k + dv * gain_v).astype(BF16).astype(F32)
         for t in range(frames):
             rows = slice(t * tt, (t + 1) * tt)
-            b_send[t, :, cols] = jnp.concatenate([direct[rows], moved[rows]], axis=0).astype(BF16)
+            b_send[t, h] = jnp.concatenate([direct[rows], moved[rows]], axis=0).astype(BF16)
         g_send[pl.ds(h, 1), :] = jnp.sum(dq * normed, axis=0, keepdims=True)
         g_send[pl.ds(heads + h, 1), :] = jnp.sum(dk * warped, axis=0, keepdims=True)
         g_send[pl.ds(2 * heads + h, 1), :] = jnp.sum(dv * warped, axis=0, keepdims=True)
         return dot_own + direct * own, dot_source + moved * source
 
     zero = jnp.zeros((count, HD), F32)
-    dot_own, dot_source = each_head(temporal_head, (zero, zero))
-
     flying = []
-    for df in range(1, frames):
-        t = at(f, df, frames)
-        flying.append(send(b_send.at[t], b_recv.at[f], b_ss.at[df], b_rs.at[df], {"frame": t}))
+    carry = (zero, zero)
+    for part, (low, high) in enumerate(groups):
+        carry = each_head(temporal_head, carry, low, high)
+        for df in range(1, frames):
+            t = at(f, df, frames)
+            flying.append(
+                send(
+                    b_send.at[t, low:high],
+                    b_recv.at[f, low:high],
+                    b_ss.at[df, part],
+                    b_rs.at[df, part],
+                    {"frame": t},
+                )
+            )
+    dot_own, dot_source = carry
     dot_own = jnp.sum(dot_own, axis=1, keepdims=True)
     dot_source = jnp.sum(dot_source, axis=1, keepdims=True)
     for t in range(frames):
@@ -274,7 +300,8 @@
     in_recv[f, m] = in_send[f]
     g_recv[c, f] = g_send[...]
     for copy in flying:
-        copy.wait()
+        copy.wait_recv()
+    sent = sent + flying + sums
 
     total = sq_recv[f, 0]
     for other in range(1, mps):
@@ -297,7 +324,7 @@
 
     def backward_head(h, carry):
         cols = head_cols(h)
-        blocks = [b_recv[j, :, cols].astype(F32) for j in range(tiles)]
+        blocks = [b_recv[j, h].astype(F32) for j in range(tiles)]
         parts = []
         for s in range(tiles):
             grad = blocks[s][:tt]
@@ -307,18 +334,18 @@
             parts.append(inverse * grad - sp_sc[s * tt : (s + 1) * tt, cols] * factor)
         upstream = jnp.concatenate(parts, axis=0).astype(BF16)
         weights = p_sc[h]
-        grad_weights = dot_nt(upstream, v_ref[:, cols])
-        inner = jnp.sum(weights * grad_weights, axis=-1, keepdims=True)
+        grad_weights = dot_nt(v_ref[:, cols], upstream)
+        inner = jnp.sum(weights * grad_weights, axis=0, keepdims=True)
         grad_scores = (weights * (grad_weights - inner) * scale).astype(BF16)
-        gq_ref[:, cols] = dot_nn(grad_scores, k_ref[:, cols]).astype(BF16)
-        gk_ref[:, cols] = dot_tn(grad_scores, q_ref[:, cols]).astype(BF16)
-        gv_ref[:, cols] = dot_tn(weights.astype(BF16), upstream).astype(BF16)
+        gq_ref[:, cols] = dot_tn(grad_scores, k_ref[:, cols]).astype(BF16)
+        gk_ref[:, cols] = dot_nn(grad_scores, q_ref[:, cols]).astype(BF16)
+        gv_ref[:, cols] = dot_nn(weights.astype(BF16), upstream).astype(BF16)
         return carry
 
     each_head(backward_head, 0)
 
     for copy in sums:
-        copy.wait()
+        copy.wait_recv()
     total = None
     for other in range(clips):
         for t in range(frames):
@@ -327,6 +354,8 @@
         for h in range(heads):
             row = g * heads + h
             gg_ref[g : g + 1, h * HD : (h + 1) * HD] = total[row : row + 1]
+    for copy in sent:
+        copy.wait_send()
 
 
 def write_out(*refs):
@@ -348,6 +377,7 @@
     table = pad8(tiles + 2)
     gain_rows = pad8(3 * heads)
     dma = pltpu.SemaphoreType.DMA
+    parts = len(cuts(heads))
     results = [((frames * tt, width), BF16)] + [((count, width), BF16)] * 3 + [((3, width), F32)]
     outs = pl.pallas_call(
         functools.partial(kernel, dims),
@@ -358,22 +388,22 @@
             pltpu.VMEM((heads, count, count), F32),
             pltpu.VMEM((count, width), F32),
             pltpu.VMEM((pad8(tiles), HD), F32),
-            pltpu.VMEM((frames, 2 * tt, width), BF16),
-            pltpu.VMEM((frames, 2 * tt, width), BF16),
+            pltpu.VMEM((frames, heads, 2 * tt, HD), BF16),
+            pltpu.VMEM((frames, heads, 2 * tt, HD), BF16),
             pltpu.VMEM((frames, table, HD), F32),
             pltpu.VMEM((frames, mps, table, HD), F32),
-            pltpu.VMEM((frames, 2 * tt, width), BF16),
-            pltpu.VMEM((frames, 2 * tt, width), BF16),
+            pltpu.VMEM((frames, heads, 2 * tt, HD), BF16),
+            pltpu.VMEM((frames, heads, 2 * tt, HD), BF16),
             pltpu.VMEM((frames, 8, HD), F32),
             pltpu.VMEM((frames, mps, 8, HD), F32),
             pltpu.VMEM((gain_rows, HD), F32),
             pltpu.VMEM((clips, frames, gain_rows, HD), F32),
-            dma((frames,)),
-            dma((frames,)),
+            dma((frames, parts)),
+            dma((frames, parts)),
             dma((frames, mps)),
             dma((frames, mps)),
-            dma((frames,)),
-            dma((frames,)),
+            dma((frames, parts)),
+            dma((frames, parts)),
             dma((frames, mps)),
             dma((frames, mps)),
             dma((clips, frames)),

time: 23.4 us -> 21.4 us (0.915)
  Pallas kernels: 22.6 us -> 20.6 us
    pallas_call x1, Pallas kernels: 21.8 us -> 19.8 us  [body(): pl.pallas_call(functools.partial(kernel, dims), out_shape=tuple((pltpu.VM...]
where the time goes in v3:
time: 21.4 us; the launch traced here: 21.3 us
  Pallas kernels  20.6 us (96%)
  between operations  0.64 us (3%)
    pallas_call x1, Pallas kernels, body(): pl.pallas_call(functools.partial(kernel, dims), out_shape=tuple((pltpu.VM...  19.8 us
    pallas_call x1, Pallas kernels, body(): pl.pallas_call(write_out, out_shape=tuple((jax.ShapeDtypeStruct(shape, ki...  0.79 us

profile of v3, /device:TPU:0, one launch (start us, length us, event | category | flops | bytes accessed | tf_op | source)
XLA Modules:
  0.0 21.3 jit_solution(9392225905499904235)
XLA Ops:
  0.6 19.8 %shard_map.101 = (bf16[80,640]{1,0:T(8,128)(2,1)S(1)}, bf16[80,640]{1,0:T(8,128)(2,1)S(1)}, bf16[80,640]{1,0:T(8,128)(2,1)S(1)}, bf16[80,640]{1,0:T(8,128)(2,1)S(1)}, f32[3,640]{1,0:T(4,128)S(1)}) custom-call(bf16[80,640]{1,0:T(8,128)(2,1)} %bitcast.11, bf16[80,640]{1,0:T(8,128)(2,1)} %bitcast.12, bf16[80,640]{1,0:T(8,128)(2,1)} %bitcast.13, ...), custom_call_target="tpu_custom_call" | custom-call | tf_op jit(solution)/shard_map/pallas_call | solution.py:382
  20.5 0.8 %shard_map.102 = (bf16[80,640]{1,0:T(8,128)(2,1)}, bf16[80,640]{1,0:T(8,128)(2,1)}, bf16[80,640]{1,0:T(8,128)(2,1)}, bf16[80,640]{1,0:T(8,128)(2,1)}, f32[3,640]{1,0:T(4,128)}) custom-call(bf16[80,640]{1,0:T(8,128)(2,1)S(1)} %get-tuple-element.15.refs_0_, bf16[80,640]{1,0:T(8,128)(2,1)S(1)} %get-tuple-element.16.refs_1_, ...), custom_call_target="tpu_custom_call" | custom-call | tf_op jit(solution)/shard_map/pallas_call | solution.py:423

commit v4 on v3

--- a/solution.py
+++ b/solution.py
@@ -44,17 +44,22 @@
 
 def kernel(
     dims,
-    q_ref,
-    k_ref,
-    v_ref,
-    gains_ref,
+    q_in,
+    k_in,
+    v_in,
+    gains_in,
     warp_ref,
-    cot_ref,
+    cot_in,
     tout_ref,
     gq_ref,
     gk_ref,
     gv_ref,
     gg_ref,
+    q_ref,
+    k_ref,
+    v_ref,
+    gains_ref,
+    cot_ref,
     p_sc,
     sp_sc,
     table_sc,
@@ -78,6 +83,7 @@
     in_rs,
     g_ss,
     g_rs,
+    load_sems,
 ):
     clips, frames, mps, tiles, tt, heads = dims
     total_width = float(heads * HD * mps)
@@ -99,6 +105,10 @@
     def in_wide(dc, df):
         return {"clip": at(c, dc, clips), "frame": at(f, df, frames)}
 
+    pairs = [(q_in, q_ref), (k_in, k_ref), (v_in, v_ref), (gains_in, gains_ref), (cot_in, cot_ref)]
+    loads = [pltpu.make_async_copy(*pair, load_sems.at[i]) for i, pair in enumerate(pairs)]
+    for load in loads:
+        load.start()
     barrier = pltpu.get_barrier_semaphore()
     peers = [in_group(*step) for step in group]
     peers += [in_wide(dc, df) for dc, df in wide if dc]
@@ -172,6 +182,8 @@
         ref[1:2, :] = source
         ref[2 : 2 + tiles, :] = table_sc[0:tiles, :]
 
+    for load in loads[:3]:
+        load.wait()
     flying = []
     squares = jnp.zeros((tiles * tt, HD), F32)
     for part, (low, high) in enumerate(groups):
@@ -207,6 +219,8 @@
         )
     tile_pair(a_recv.at[f], f, 0, heads)
     sq_recv[f, m] = sq_send[0]
+    for load in loads[3:]:
+        load.wait()
     for copy in flying:
         copy.wait_recv()
     sent = flying
@@ -374,6 +388,7 @@
     count = tiles * tt
     dims = (clips, frames, mps, tiles, tt, heads)
     vmem = pl.BlockSpec(memory_space=pltpu.VMEM)
+    far = pl.BlockSpec(memory_space=pl.ANY)
     table = pad8(tiles + 2)
     gain_rows = pad8(3 * heads)
     dma = pltpu.SemaphoreType.DMA
@@ -382,9 +397,14 @@
     outs = pl.pallas_call(
         functools.partial(kernel, dims),
         out_shape=tuple(pltpu.VMEM(shape, kind) for shape, kind in results),
-        in_specs=[vmem, vmem, vmem, vmem, pl.BlockSpec(memory_space=pltpu.SMEM), vmem],
+        in_specs=[far, far, far, far, pl.BlockSpec(memory_space=pltpu.SMEM), far],
         out_specs=(vmem,) * 5,
         scratch_shapes=[
+            pltpu.VMEM((count, width), BF16),
+            pltpu.VMEM((count, width), BF16),
+            pltpu.VMEM((count, width), BF16),
+            pltpu.VMEM((3, width), F32),
+            pltpu.VMEM((frames * tt, width), BF16),
             pltpu.VMEM((heads, count, count), F32),
             pltpu.VMEM((count, width), F32),
             pltpu.VMEM((pad8(tiles), HD), F32),
@@ -408,6 +428,7 @@
             dma((frames, mps)),
             dma((clips, frames)),
             dma((clips, frames)),
+            dma((5,)),
         ],
         compiler_params=pltpu.CompilerParams(
             collective_id=0, has_side_effects=True, vmem_limit_bytes=56 * 2**20

time: 21.4 us -> 21.1 us (0.986)
  Pallas kernels: 20.6 us -> 20.3 us
    pallas_call x1, Pallas kernels: 19.8 us -> 19.5 us  [body(): pl.pallas_call(functools.partial(kernel, dims), out_shape=tuple((pltpu.VM...]
where the time goes in v4:
time: 21.1 us; the launch traced here: 20.9 us
  Pallas kernels  20.3 us (96%)
  between operations  0.64 us (3%)
    pallas_call x1, Pallas kernels, body(): pl.pallas_call(functools.partial(kernel, dims), out_shape=tuple((pltpu.VM...  19.5 us
    pallas_call x1, Pallas kernels, body(): pl.pallas_call(write_out, out_shape=tuple((jax.ShapeDtypeStruct(shape, ki...  0.79 us

profile of v4, /device:TPU:0, one launch (start us, length us, event | category | flops | bytes accessed | tf_op | source)
XLA Modules:
  0.0 20.9 jit_solution(15104064094539034763)
XLA Ops:
  0.6 19.5 %shard_map.101 = (bf16[80,640]{1,0:T(8,128)(2,1)S(1)}, bf16[80,640]{1,0:T(8,128)(2,1)S(1)}, bf16[80,640]{1,0:T(8,128)(2,1)S(1)}, bf16[80,640]{1,0:T(8,128)(2,1)S(1)}, f32[3,640]{1,0:T(4,128)S(1)}) custom-call(bf16[80,640]{1,0:T(8,128)(2,1)} %bitcast.11, bf16[80,640]{1,0:T(8,128)(2,1)} %bitcast.12, bf16[80,640]{1,0:T(8,128)(2,1)} %bitcast.13, ...), custom_call_target="tpu_custom_call" | custom-call | tf_op jit(solution)/shard_map/pallas_call | solution.py:397
  20.1 0.8 %shard_map.102 = (bf16[80,640]{1,0:T(8,128)(2,1)}, bf16[80,640]{1,0:T(8,128)(2,1)}, bf16[80,640]{1,0:T(8,128)(2,1)}, bf16[80,640]{1,0:T(8,128)(2,1)}, f32[3,640]{1,0:T(4,128)}) custom-call(bf16[80,640]{1,0:T(8,128)(2,1)S(1)} %get-tuple-element.15.refs_0_, bf16[80,640]{1,0:T(8,128)(2,1)S(1)} %get-tuple-element.16.refs_1_, ...), custom_call_target="tpu_custom_call" | custom-call | tf_op jit(solution)/shard_map/pallas_call | solution.py:444
